TPU v7x, 32 devices: a whole 2x2x4 slice. The times are simulated.
32 devices in a mesh: dp: 8 (over z, y), shard: 4 (over x, core).
Axes of the slice: x: 2, y: 2, z: 4, core: 2. Of those that a mesh axis runs over, the one named last changes fastest.
Arguments:
- char_ids: int32 [2048, 4], P(('dp', 'shard')), may hold values from 0 to 274
- targets: int32 [2048, 4], P(('dp', 'shard')), may hold values from 0 to 274
- hidden_start: float32 [2048, 2048], P(('dp', 'shard')), may hold values from -0.9 to 0.9
- cell_start: float32 [2048, 2048], P(('dp', 'shard')), may hold values from -4 to 4
- embedding: float32 [275, 100], replicated, may hold values from -5 to 5
- input_weight: float32 [8192, 100], P(('dp', 'shard')), may hold values from -0.625 to 0.625
- hidden_weight: float32 [8192, 2048], P(('dp', 'shard')), may hold values from -0.125 to 0.125
- gate_bias: float32 [8192], P(('dp', 'shard')), may hold values from -3 to 3
- decoder_weight: float32 [2048, 275], P(('dp', 'shard')), may hold values from -0.5 to 0.5
- decoder_bias: float32 [275], replicated, may hold values from -3 to 3
- momentum_embed: float32 [275, 100], replicated, may hold values from -0.0008544922 to 0.0008544922
- momentum_input: float32 [8192, 100], P(('dp', 'shard')), may hold values from -0.001953125 to 0.001953125
- momentum_hidden: float32 [8192, 2048], P(('dp', 'shard')), may hold values from -0.00061035156 to 0.00061035156
- momentum_gate: float32 [8192], P(('dp', 'shard')), may hold values from -0.0078125 to 0.0078125
- momentum_decoder: float32 [2048, 275], P(('dp', 'shard')), may hold values from -0.00390625 to 0.00390625
- momentum_outbias: float32 [275], replicated, may hold values from -0.75 to 0.75
Outputs:
- loss: float32 [1], replicated
- grad_norm: float32 [1], replicated
- grad_hidden_start: float32 [2048, 2048], P(('dp', 'shard'))
- grad_cell_start: float32 [2048, 2048], P(('dp', 'shard'))
- grad_embedding: float32 [275, 100], replicated
- grad_input_weight: float32 [8192, 100], P(('dp', 'shard'))
- grad_hidden_weight: float32 [8192, 2048], P(('dp', 'shard'))
- grad_gate_bias: float32 [8192], P(('dp', 'shard'))
- grad_decoder_weight: float32 [2048, 275], P(('dp', 'shard'))
- grad_decoder_bias: float32 [275], replicated
- new_momentum_embed: float32 [275, 100], replicated
- new_momentum_input: float32 [8192, 100], P(('dp', 'shard'))
- new_momentum_hidden: float32 [8192, 2048], P(('dp', 'shard'))
- new_momentum_gate: float32 [8192], P(('dp', 'shard'))
- new_momentum_decoder: float32 [2048, 275], P(('dp', 'shard'))
- new_momentum_outbias: float32 [275], replicated
All inputs are finite; a program needn't handle non-finite values.
Results may differ from a plain program's by a relative error of at most 0.0097.
Values may be sent and summed in bfloat16 or wider, within the bound.
A program may use at most 192 MiB of HBM per device.

v0:
```python
import functools

import jax
import jax.numpy as jnp
from jax import lax
from jax.experimental import pallas as pl
from jax.experimental.pallas import tpu as pltpu
from jax.sharding import PartitionSpec as P

MESH = pl.DeviceIdType.MESH
F32 = jnp.float32
BF16 = jnp.bfloat16

MICRO = 2


CLIP = 0.25
MOMENTUM = 0.5


def contract_rows(left, right):
    return lax.dot_general(
        left, right, (((0,), (0,)), ((), ())), preferred_element_type=jnp.float32
    )


def contract_last(left, right):
    return lax.dot_general(
        left, right, (((1,), (1,)), ((), ())), preferred_element_type=jnp.float32
    )


def local(
    char_ids,
    targets,
    hidden_start,
    cell_start,
    embedding,
    input_weight,
    hidden_weight,
    gate_bias,
    decoder_weight,
    decoder_bias,
    momentum_embed,
    momentum_input,
    momentum_hidden,
    momentum_gate,
    momentum_decoder,
    momentum_outbias,
):
    streams, seq_len = char_ids.shape
    micro_rows = streams // MICRO
    vocab_size = embedding.shape[0]
    hidden_size = hidden_start.shape[1]
    low_input = input_weight.astype(jnp.bfloat16)
    low_hidden = hidden_weight.astype(jnp.bfloat16)
    low_bias = gate_bias.astype(jnp.bfloat16)
    low_decoder = decoder_weight.astype(jnp.bfloat16)
    inner_rows = (
        lax.all_gather(low_input, "shard", axis=0, tiled=True),
        lax.all_gather(low_hidden, "shard", axis=0, tiled=True),
        lax.all_gather(low_bias, "shard", axis=0, tiled=True),
        lax.all_gather(low_decoder, "shard", axis=0, tiled=True),
    )
    weight_in, weight_rec, bias_low, weight_out = (
        lax.all_gather(inner_rows[0], "dp", axis=0, tiled=True),
        lax.all_gather(inner_rows[1], "dp", axis=0, tiled=True),
        lax.all_gather(inner_rows[2], "dp", axis=0, tiled=True),
        lax.all_gather(inner_rows[3], "dp", axis=0, tiled=True),
    )
    columns = jnp.arange(vocab_size, dtype=jnp.int32)
    table = embedding.astype(jnp.bfloat16)
    bias_row = bias_low.astype(jnp.float32)[None, :]

    def forward_step(carried, input_now):
        hidden_low, cell = carried
        preact = input_now + contract_last(hidden_low, weight_rec)
        input_gate = jax.nn.sigmoid(preact[:, :hidden_size])
        forget_gate = jax.nn.sigmoid(preact[:, hidden_size : 2 * hidden_size])
        candidate = jnp.tanh(preact[:, 2 * hidden_size : 3 * hidden_size])
        output_gate = jax.nn.sigmoid(preact[:, 3 * hidden_size :])
        cell_next = forget_gate * cell + input_gate * candidate
        hidden_next = (output_gate * jnp.tanh(cell_next)).astype(jnp.bfloat16)
        activations = jnp.concatenate([input_gate, forget_gate, candidate, output_gate], axis=1)
        return ((hidden_next, cell_next), (hidden_low, cell, activations, cell_next, hidden_next))

    def backward_step(carried, inputs):
        hidden_grad_next, cell_grad_next = carried
        out_grad, cell_before, gate_values, cell_now = inputs
        hidden_grad = out_grad + hidden_grad_next
        input_gate = gate_values[:, :hidden_size]
        forget_gate = gate_values[:, hidden_size : 2 * hidden_size]
        candidate = gate_values[:, 2 * hidden_size : 3 * hidden_size]
        output_gate = gate_values[:, 3 * hidden_size :]
        cell_tanh = jnp.tanh(cell_now)
        cell_grad = cell_grad_next + hidden_grad * output_gate * (1.0 - cell_tanh * cell_tanh)
        input_term = cell_grad * candidate * input_gate * (1.0 - input_gate)
        forget_term = cell_grad * cell_before * forget_gate * (1.0 - forget_gate)
        candidate_term = cell_grad * input_gate * (1.0 - candidate * candidate)
        output_term = hidden_grad * cell_tanh * output_gate * (1.0 - output_gate)
        gate_grad = jnp.concatenate(
            [input_term, forget_term, candidate_term, output_term], axis=1
        ).astype(jnp.bfloat16)
        hidden_grad_prev = jnp.dot(gate_grad, weight_rec, preferred_element_type=jnp.float32)
        return ((hidden_grad_prev, cell_grad * forget_gate), gate_grad)

    def micro_pass(loss_total, inputs):
        ids_part, target_part, hidden_part, cell_part = inputs
        batch_rows = ids_part.shape[0]
        token_ids = ids_part.T.reshape(-1)
        token_targets = target_part.T.reshape(-1)
        one_input = (token_ids[:, None] == columns[None, :]).astype(jnp.bfloat16)
        one_target = (token_targets[:, None] == columns[None, :]).astype(jnp.float32)
        embedded = jnp.dot(one_input, table, preferred_element_type=jnp.float32).astype(
            jnp.bfloat16
        )
        input_part = contract_last(embedded, weight_in) + bias_row
        input_part = input_part.reshape(seq_len, batch_rows, 4 * hidden_size)
        start_pair = (hidden_part.astype(jnp.bfloat16), cell_part)
        final_pair, saved = lax.scan(forward_step, start_pair, input_part)
        hidden_prev, cell_prev, activations, cell_after, hidden_after = saved
        hidden_rows = hidden_after.reshape(seq_len * batch_rows, hidden_size)
        logits = (
            jnp.dot(hidden_rows, weight_out, preferred_element_type=jnp.float32)
            + decoder_bias[None, :]
        )
        log_total = jax.nn.logsumexp(logits, axis=1)
        local_loss = jnp.sum(log_total - jnp.sum(one_target * logits, axis=1)) / seq_len
        probs = jnp.exp(logits - log_total[:, None])
        logit_grad = ((probs - one_target) / seq_len).astype(jnp.bfloat16)
        hidden_from_out = contract_last(logit_grad, weight_out).reshape(
            seq_len, batch_rows, hidden_size
        )
        zero_state = jnp.zeros((batch_rows, hidden_size), jnp.float32)
        start_grads, gate_grads = lax.scan(
            backward_step,
            (zero_state, zero_state),
            (hidden_from_out, cell_prev, activations, cell_after),
            reverse=True,
        )
        gate_rows = gate_grads.reshape(seq_len * batch_rows, 4 * hidden_size)
        prev_rows = hidden_prev.reshape(seq_len * batch_rows, hidden_size)
        return (
            loss_total + local_loss,
            (
                token_ids,
                embedded,
                logit_grad,
                hidden_rows,
                gate_rows,
                prev_rows,
                start_grads[0],
                start_grads[1],
            ),
        )

    def by_micro(array):
        return array.reshape((MICRO, micro_rows) + array.shape[1:])

    local_loss, stacked = lax.scan(
        micro_pass,
        jnp.zeros((), jnp.float32),
        (by_micro(char_ids), by_micro(targets), by_micro(hidden_start), by_micro(cell_start)),
    )
    token_ids, embedded, logit_grad, hidden_rows, gate_rows, prev_rows, hidden_grads, cell_grads = (
        stacked
    )
    token_ids = token_ids.reshape(-1)
    embedded = embedded.reshape(-1, embedded.shape[-1])
    logit_grad = logit_grad.reshape(-1, vocab_size)
    hidden_rows = hidden_rows.reshape(-1, hidden_size)
    gate_rows = gate_rows.reshape(-1, 4 * hidden_size)
    prev_rows = prev_rows.reshape(-1, hidden_size)
    grad_hidden_start = hidden_grads.reshape(streams, hidden_size)
    grad_cell_start = cell_grads.reshape(streams, hidden_size)
    grad_outbias_local = jnp.sum(logit_grad.astype(jnp.float32), axis=0)
    grad_decoder_local = contract_rows(hidden_rows, logit_grad)
    grad_input_local = contract_rows(gate_rows, embedded)
    grad_hidden_local = contract_rows(gate_rows, prev_rows)
    grad_bias_local = jnp.sum(gate_rows.astype(jnp.float32), axis=0)
    embed_rows_grad = jnp.dot(gate_rows, weight_in, preferred_element_type=jnp.float32)
    one_all = (token_ids[:, None] == columns[None, :]).astype(jnp.float32)
    grad_embed_local = lax.dot_general(
        one_all,
        embed_rows_grad,
        (((0,), (0,)), ((), ())),
        precision=lax.Precision.HIGHEST,
        preferred_element_type=jnp.float32,
    )
    grad_embedding, grad_decoder_bias, loss_sum = lax.psum(
        (grad_embed_local, grad_outbias_local, local_loss), ("dp", "shard")
    )
    outer_sums = (
        lax.psum_scatter(
            grad_input_local.astype(jnp.bfloat16), "dp", scatter_dimension=0, tiled=True
        ).astype(jnp.float32),
        lax.psum_scatter(
            grad_hidden_local.astype(jnp.bfloat16), "dp", scatter_dimension=0, tiled=True
        ).astype(jnp.float32),
        lax.psum_scatter(
            grad_bias_local.astype(jnp.bfloat16), "dp", scatter_dimension=0, tiled=True
        ).astype(jnp.float32),
        lax.psum_scatter(
            grad_decoder_local.astype(jnp.bfloat16), "dp", scatter_dimension=0, tiled=True
        ).astype(jnp.float32),
    )
    grad_input_weight, grad_hidden_weight, grad_gate_bias, grad_decoder_weight = (
        lax.psum_scatter(
            outer_sums[0].astype(jnp.bfloat16), "shard", scatter_dimension=0, tiled=True
        ).astype(jnp.float32),
        lax.psum_scatter(
            outer_sums[1].astype(jnp.bfloat16), "shard", scatter_dimension=0, tiled=True
        ).astype(jnp.float32),
        lax.psum_scatter(
            outer_sums[2].astype(jnp.bfloat16), "shard", scatter_dimension=0, tiled=True
        ).astype(jnp.float32),
        lax.psum_scatter(
            outer_sums[3].astype(jnp.bfloat16), "shard", scatter_dimension=0, tiled=True
        ).astype(jnp.float32),
    )
    shard_squares = jnp.sum(grad_input_weight * grad_input_weight) + jnp.sum(
        grad_hidden_weight * grad_hidden_weight
    )
    shard_squares = (
        shard_squares
        + jnp.sum(grad_gate_bias * grad_gate_bias)
        + jnp.sum(grad_decoder_weight * grad_decoder_weight)
    )
    square_total = lax.psum(shard_squares, ("dp", "shard"))
    square_total = (
        square_total
        + jnp.sum(grad_embedding * grad_embedding)
        + jnp.sum(grad_decoder_bias * grad_decoder_bias)
    )
    grad_norm = jnp.sqrt(square_total)
    factor = CLIP / jnp.maximum(grad_norm, CLIP)
    streams_all = streams * lax.axis_size("dp") * lax.axis_size("shard")
    loss = loss_sum / streams_all
    momenta = (
        momentum_embed,
        momentum_input,
        momentum_hidden,
        momentum_gate,
        momentum_decoder,
        momentum_outbias,
    )
    weight_grads = (
        grad_embedding,
        grad_input_weight,
        grad_hidden_weight,
        grad_gate_bias,
        grad_decoder_weight,
        grad_decoder_bias,
    )
    new_momenta = [MOMENTUM * momenta[index] + factor * weight_grads[index] for index in range(6)]
    return (
        loss.reshape(1),
        grad_norm.reshape(1),
        grad_hidden_start,
        grad_cell_start,
        grad_embedding,
        grad_input_weight,
        grad_hidden_weight,
        grad_gate_bias,
        grad_decoder_weight,
        grad_decoder_bias,
        new_momenta[0],
        new_momenta[1],
        new_momenta[2],
        new_momenta[3],
        new_momenta[4],
        new_momenta[5],
    )


ROWS = 256
HID = 2048
WIDE = 2176
INPUTS = 100
CHARS = 384
SPLIT = 2
PART = ROWS // SPLIT
SLICES = 8
SLICE = ROWS // SLICES
STEPS = 4


def spots():
    dp = lax.axis_index("dp")
    shard = lax.axis_index("shard")
    return dict(
        p=dp // 4,
        zi=(dp // 2) % 2,
        z=dp // 2,
        y=dp % 2,
        k=dp % 4,
        x=shard // 2,
        c=shard % 2,
        dp=dp,
        shard=shard,
    )


def device(s, z=None, y=None, x=None, c=None):
    z = s["z"] if z is None else z
    y = s["y"] if y is None else y
    x = s["x"] if x is None else x
    c = s["c"] if c is None else c
    return (z * 2 + y, x * 2 + c)


def peer(s, d):
    y = 1 - s["y"] if d % 2 else s["y"]
    zi = 1 - s["zi"] if d // 2 else s["zi"]
    z = 2 * s["p"] + zi
    return dict(y=y, zi=zi, k=2 * zi + y, dev=(z * 2 + y, s["shard"]))


def stripe(y, zi, xb):
    return 4 * y + 2 * xb + zi


def cols(index):
    return pl.ds(pl.multiple_of(index * ROWS, ROWS), ROWS)


def aligned(start, size):
    return pl.ds(pl.multiple_of(start, size), size)


def remote(src, dst, send, recv, dev):
    return pltpu.make_async_remote_copy(
        src_ref=src, dst_ref=dst, send_sem=send, recv_sem=recv, device_id=dev, device_id_type=MESH
    )


def dot(left, right):
    return jnp.dot(left, right, preferred_element_type=F32)


def dot_nt(left, right):
    return lax.dot_general(left, right, (((1,), (1,)), ((), ())), preferred_element_type=F32)


def dot_tn(left, right):
    return lax.dot_general(left, right, (((0,), (0,)), ((), ())), preferred_element_type=F32)


def signal(dev):
    pl.semaphore_signal(
        pltpu.get_barrier_semaphore(), inc=1, device_id=dev, device_id_type=MESH
    )


def step_kernel(
    wext,
    h_own,
    cell_own,
    meta_own,
    wout_own,
    table,
    dbias,
    hx_o,
    dg_o,
    dh0_o,
    dc0_o,
    emb_o,
    gdec_o,
    w2,
    wt,
    hx,
    act,
    call,
    dg,
    pbuf,
    rbuf,
    ownp,
    dcn,
    wo,
    dlog,
    metas,
    emb,
    cells,
    dpart,
    d_out,
    d_in,
    f_out,
    f_in,
    g_send,
    g_recv,
    wz_send,
    wz_recv,
    wx_send,
    wx_recv,
    wc_send,
    wc_recv,
    o_send,
    o_recv,
    h_send,
    h_recv,
    b_send,
    b_recv,
    d_send,
    d_recv,
    f_send,
    f_recv,
    out_sem,
):
    s = spots()
    z, y, x, c, k, zi, p = s["z"], s["y"], s["x"], s["c"], s["k"], s["zi"], s["p"]
    dp, shard = s["dp"], s["shard"]
    across = device(s, x=1 - x)
    twin = device(s, c=1 - c)
    far = device(s, z=2 * (1 - p) + zi)
    peers = {d: peer(s, d) for d in (1, 2, 3)}
    mine = [stripe(y, zi, xb) for xb in (0, 1)]
    core = z % 2
    off_core = jnp.where(core == c, 0, 1)
    quad = [(dx, dc) for dx in range(2) for dc in range(2) if (dx, dc) != (0, 0)]

    def flip(value, by):
        return 1 - value if by else value

    def quad_to(dx, dc):
        return device(s, x=flip(x, dx), c=flip(c, dc))

    def final_to(xb):
        return 4 * y + 2 * xb + zi

    def final_from(half):
        return 4 * half + 2 * y + p

    for d in (1, 2, 3):
        signal(peers[d]["dev"])
    signal(across)
    signal(twin)
    signal(far)

    signal(device(s, x=1 - x, c=1 - c))

    @pl.when(core != c)
    def _():
        for i in (0, 1):
            signal(device(s, z=c + 2 * i, c=core))

    away = 0
    for n in (0, 1):

        @pl.when(final_from(n) != dp)
        def _():
            signal((final_from(n), shard))

        away = away + jnp.where(final_to(n) != dp, 1, 0)
    pl.semaphore_wait(pltpu.get_barrier_semaphore(), 7 + 2 * off_core + away)

    def z_copy(target, q):
        rows = pl.ds(q * SLICE, SLICE)
        slot = aligned((2 * z + x) * ROWS + q * SLICE, SLICE)
        return remote(
            wext.at[rows],
            w2.at[slot],
            wz_send.at[target, q],
            wz_recv.at[z // 2, q],
            device(s, z=c + 2 * target, c=core),
        )

    def z_wait(i, q):
        slot = aligned((2 * (c + 2 * i) + x) * ROWS + q * SLICE, SLICE)
        remote(wext.at[pl.ds(q * SLICE, SLICE)], w2.at[slot], wz_send.at[0, q], wz_recv.at[i, q], across).wait_recv()

    def x_copy(i, q, sender=True):
        xs = x if sender else 1 - x
        slot = aligned((2 * (c + 2 * i) + xs) * ROWS + q * SLICE, SLICE)
        return remote(w2.at[slot], w2.at[slot], wx_send.at[i, q], wx_recv.at[i, q], across)

    def c_copy(i, q, n, other, sender=True):
        xs = 1 - x if other else x
        cs = c if sender else 1 - c
        slot = aligned((2 * (cs + 2 * i) + xs) * ROWS + q * SLICE, SLICE)
        return remote(
            w2.at[slot], w2.at[slot], wc_send.at[n, int(other), q], wc_recv.at[n, int(other), q], twin
        )

    near = p
    beyond = 1 - p

    def start_beyond():
        for q in range(SLICES):

            @pl.when(c + 2 * beyond != z)
            def _():
                z_copy(beyond, q).start()

    pl.when(zi != p)(start_beyond)
    own = aligned(k * 64, 64)

    def group_copy(d, n):
        dev = peers[d]["dev"]
        send, recv = g_send.at[d - 1, n], g_recv.at[d - 1, n]
        if n == 0:
            return remote(meta_own, metas.at[own], send, recv, dev)
        if n == 1:
            return remote(h_own, hx.at[0, own, pl.ds(0, HID)], send, recv, dev)
        if n == 2:
            return remote(wout_own, wo.at[dp, shard], send, recv, dev)
        theirs = stripe(peers[d]["y"], peers[d]["zi"], n - 3)
        return remote(cell_own.at[:, cols(theirs)], cells.at[n - 3, own], send, recv, dev)

    def corner_copy(n, sender=True):
        there = peers[2 if sender else 3]
        rows = aligned(there["k"] * 64, 64)
        send, recv = g_send.at[2, n], g_recv.at[2, n]
        dev = peers[1]["dev"]
        if n == 0:
            part = metas.at[rows]
        elif n == 1:
            part = hx.at[0, rows, pl.ds(0, HID)]
        else:
            part = wo.at[there["dev"][0], shard]
        return remote(part, part, send, recv, dev)

    @pl.when(c + 2 * near == z)
    def _():
        w2[aligned((2 * z + x) * ROWS, ROWS), :] = wext[...]

    for q in range(SLICES):

        @pl.when(c + 2 * near != z)
        def _():
            z_copy(near, q).start()

        if q == 0:
            for n in (0, 2, 1):
                for d in (2, 1):
                    group_copy(d, n).start()
    for n in (3, 4):
        for d in (3, 2, 1):
            group_copy(d, n).start()
    pl.when(zi == p)(start_beyond)
    metas[own, :] = meta_own[...]
    hx[0, own, pl.ds(0, HID)] = h_own[...]
    wo[dp, shard] = wout_own[...]
    for xb in (0, 1):
        cells[xb, own] = cell_own[:, cols(mine[xb])]

    def group_wait(d, n):
        there = peers[d]
        rows = aligned(there["k"] * 64, 64)
        send, recv = g_send.at[d - 1, n], g_recv.at[d - 1, n]
        if n == 0:
            copy = remote(meta_own, metas.at[rows], send, recv, there["dev"])
        elif n == 1:
            copy = remote(h_own, hx.at[0, rows, pl.ds(0, HID)], send, recv, there["dev"])
        elif n == 2:
            copy = remote(wout_own, wo.at[there["dev"][0], shard], send, recv, there["dev"])
        else:
            copy = remote(cell_own.at[:, cols(mine[n - 3])], cells.at[n - 3, rows], send, recv, there["dev"])
        copy.wait_recv()

    lanes = lax.broadcasted_iota(jnp.int32, (ROWS, CHARS), 1)

    def turn(b):
        wt[b] = w2[cols(b), :].T

    order = [(n, q) for n in (0, 1) for q in range(SLICES)]
    gates = (p, 1 - p)
    for at, (n, q) in enumerate(order):
        i = gates[n]

        @pl.when(c + 2 * i != z)
        def _():
            z_wait(i, q)

        x_copy(i, q).start()
        c_copy(i, q, n, False).start()
        if at > 0:
            before, slot = order[at - 1]
            x_copy(gates[before], slot, False).wait_recv()
            c_copy(gates[before], slot, before, True).start()
        if n == 0 and q == SLICES - 1:
            for m in (0, 2, 1):
                group_wait(2, m)
                corner_copy(m).start()
        if n == 1 and q < 2:
            turn(2 * (c + 2 * p) + q)
        if n == 1 and q == 2:
            for other in (False, True):
                for slot in range(SLICES):
                    c_copy(p, slot, 0, other, False).wait_recv()
            for xs in (0, 1):
                turn(2 * (1 - c + 2 * p) + xs)
    x_copy(1 - p, SLICES - 1, False).wait_recv()
    c_copy(1 - p, SLICES - 1, 1, True).start()
    for xs in (0, 1):
        turn(2 * (c + 2 * (1 - p)) + xs)
    for other in (False, True):
        for q in range(SLICES):
            c_copy(1 - p, q, 1, other, False).wait_recv()
    for xs in (0, 1):
        turn(2 * (1 - c + 2 * (1 - p)) + xs)
    for n in (0, 1, 2):
        group_wait(1, n)
        corner_copy(n, False).wait_recv()
    for n in (3, 4):
        for d in (1, 2, 3):
            group_wait(d, n)
        call[0, n - 3] = cells[n - 3].astype(F32)
    for t in range(STEPS):
        one = jnp.where(metas[:, t : t + 1] == lanes, 1.0, 0.0).astype(BF16)
        hx[t, :, pl.ds(HID, WIDE - HID)] = dot(one, table[...]).astype(BF16)

    def far_copy(sender=True):
        first = 4 * p if sender else 4 * (1 - p)
        part = wo.at[pl.ds(first, 4), shard]
        return remote(part, part, o_send.at[0], o_recv.at[0], far)

    def over_copy(sender=True):
        part = wo.at[:, 2 * x + c if sender else 2 * (1 - x) + c]
        return remote(part, part, o_send.at[1], o_recv.at[1], across)

    def twin_copy(xs, sender=True):
        part = wo.at[:, 2 * xs + (c if sender else 1 - c)]
        return remote(part, part, o_send.at[2 + xs], o_recv.at[2 + xs], twin)

    def h_copy(t, part, xb, d, sender=True):
        there = peers[d]
        rows = pl.ds(part * PART, PART)
        at = mine[xb] if sender else stripe(there["y"], there["zi"], xb)
        block = hx.at[t + 1, rows, cols(at)]
        return remote(block, block, h_send.at[t, part, xb, d - 1], h_recv.at[t, part, xb, d - 1], there["dev"])

    def forward(t, part):
        rows = pl.ds(part * PART, PART)
        for xb in (0, 1):

            def pre(g):
                return dot(hx[t, rows, :], wt[2 * g + xb])

            gate_i = jax.nn.sigmoid(pre(0))
            act[t, xb, rows] = gate_i
            gate_f = jax.nn.sigmoid(pre(1))
            act[t, 2 + xb, rows] = gate_f
            gate_g = jnp.tanh(pre(2))
            act[t, 4 + xb, rows] = gate_g
            gate_o = jax.nn.sigmoid(pre(3))
            act[t, 6 + xb, rows] = gate_o
            cell = gate_f * call[t, xb, rows] + gate_i * gate_g
            call[t + 1, xb, rows] = cell
            hx[t + 1, rows, cols(mine[xb])] = (gate_o * jnp.tanh(cell)).astype(BF16)
            for d in (3, 1, 2):
                h_copy(t, part, xb, d).start()

    def h_wait(t, part):
        for xb in (0, 1):
            for d in (1, 2, 3):
                h_copy(t, part, xb, d, False).wait_recv()

    part_lanes = lax.broadcasted_iota(jnp.int32, (PART, CHARS), 1)
    part_rows = lax.broadcasted_iota(jnp.int32, (PART, 1), 0)
    totals = dict(loss=jnp.zeros((1, 1), F32), bias=jnp.zeros((1, CHARS), F32))

    def decode(t, part):
        rows = pl.ds(part * PART, PART)
        logits = dot(hx[t + 1, rows, pl.ds(0, HID)], wo[...].reshape(HID, CHARS)) + dbias[0:1, :]
        top = jnp.max(logits, axis=1, keepdims=True)
        grown = jnp.exp(logits - top)
        total = jnp.sum(grown, axis=1, keepdims=True)
        hit = metas[rows, STEPS + t : STEPS + t + 1] == part_lanes
        picked = jnp.sum(jnp.where(hit, logits, 0.0), axis=1, keepdims=True)
        low = ((grown / total - jnp.where(hit, 1.0, 0.0)) / STEPS).astype(BF16)
        dlog[t, rows] = low
        at = part_rows + part * PART
        ours = (at >= k * 64) & (at < k * 64 + 64)
        term = jnp.where(ours, (top + jnp.log(total) - picked) / STEPS, 0.0)
        totals["loss"] = totals["loss"] + jnp.sum(term, axis=0, keepdims=True)
        totals["bias"] = totals["bias"] + jnp.sum(jnp.where(ours, low.astype(F32), 0.0), axis=0, keepdims=True)

    far_copy().start()
    for part in range(SPLIT):
        forward(0, part)
    far_copy(False).wait_recv()
    over_copy().start()
    for part in range(SPLIT):
        h_wait(0, part)
        forward(1, part)
    over_copy(False).wait_recv()
    for xs in (0, 1):
        twin_copy(xs).start()
    for part in range(SPLIT):
        h_wait(1, part)
        forward(2, part)
    for xs in (0, 1):
        twin_copy(xs, False).wait_recv()
    for part in range(SPLIT):
        decode(0, part)
    for part in range(SPLIT):
        h_wait(2, part)
        forward(3, part)
    for part in range(SPLIT):
        decode(1, part)
    hx_out = pltpu.make_async_copy(hx.at[pl.ds(0, STEPS)], hx_o, out_sem.at[0])
    hx_out.start()
    for part in range(SPLIT):
        decode(2, part)

    emb[...] = jnp.zeros_like(emb)
    dcn[...] = jnp.zeros_like(dcn)

    def b_copy(t, part, d):
        rows = pl.ds(part * PART, PART)
        return remote(
            pbuf.at[t - 1, d - 1, rows],
            rbuf.at[t - 1, d - 1, rows],
            b_send.at[t - 1, part, d - 1],
            b_recv.at[t - 1, part, d - 1],
            peers[d]["dev"],
        )

    def backward(t, part):
        rows = pl.ds(part * PART, PART)
        if t < STEPS - 1:
            for d in (1, 2, 3):
                b_copy(t + 1, part, d).wait_recv()
        for xb in (0, 1):
            dh = dot_nt(dlog[t, rows], wo[mine[xb]].reshape(ROWS, CHARS))
            wide = pl.ds(xb * ROWS, ROWS)
            if t < STEPS - 1:
                dh = dh + ownp[rows, wide]
                for d in (1, 2, 3):
                    dh = dh + rbuf[t, d - 1, rows, wide].astype(F32)
            gate_i = act[t, xb, rows]
            gate_f = act[t, 2 + xb, rows]
            gate_g = act[t, 4 + xb, rows]
            gate_o = act[t, 6 + xb, rows]
            shown = jnp.tanh(call[t + 1, xb, rows])
            dc = dcn[xb, rows] + dh * gate_o * (1.0 - shown * shown)
            dcn[xb, rows] = dc * gate_f
            dg[t, rows, pl.ds(xb * ROWS, ROWS)] = (dc * gate_g * gate_i * (1.0 - gate_i)).astype(BF16)
            dg[t, rows, pl.ds((2 + xb) * ROWS, ROWS)] = (
                dc * call[t, xb, rows] * gate_f * (1.0 - gate_f)
            ).astype(BF16)
            dg[t, rows, pl.ds((4 + xb) * ROWS, ROWS)] = (dc * gate_i * (1.0 - gate_g * gate_g)).astype(BF16)
            dg[t, rows, pl.ds((6 + xb) * ROWS, ROWS)] = (dh * shown * gate_o * (1.0 - gate_o)).astype(BF16)
        if t > 0:
            for d in (3, 1, 2):
                there = peers[d]
                for xb in (0, 1):
                    pbuf[t - 1, d - 1, rows, pl.ds(xb * ROWS, ROWS)] = dot(
                        dg[t, rows, :], w2[:, cols(stripe(there["y"], there["zi"], xb))]
                    ).astype(BF16)
                b_copy(t, part, d).start()
            for xb in (0, 1):
                ownp[rows, pl.ds(xb * ROWS, ROWS)] = dot(dg[t, rows, :], w2[:, cols(mine[xb])])
        else:

            def unit(j, carry):
                dh0_o[rows, cols(j)] = dot(dg[0, rows, :], w2[:, cols(j)])
                return carry

            lax.fori_loop(0, HID // ROWS, unit, 0)

    def extras(t):
        dx = dot(dg[t], w2[:, pl.ds(HID, WIDE - HID)])
        high = dx.astype(BF16)
        rest = (dx - high.astype(F32)).astype(BF16)
        one = jnp.where(metas[:, t : t + 1] == lanes, 1.0, 0.0).astype(BF16)
        emb[...] += dot_tn(one, high) + dot_tn(one, rest)

    def d_copy(n):
        return remote(d_out.at[n], d_in.at[n], d_send.at[n], d_recv.at[n], quad_to(*quad[n]))

    def f_copy(xb):
        return remote(f_out.at[xb], f_in.at[p], f_send.at[xb], f_recv.at[p], (final_to(xb), shard))

    def f_wait(n):
        remote(f_out.at[n], f_in.at[n], f_send.at[n], f_recv.at[n], across).wait_recv()

    def decoder_start():
        for xb in (0, 1):
            total = dot_tn(hx[1, :, cols(mine[xb])], dlog[0])
            for t in range(1, STEPS):
                total = total + dot_tn(hx[t + 1, :, cols(mine[xb])], dlog[t])
            dpart[xb] = total
        for n, (dx, dc) in enumerate(quad):
            theirs = 2 * flip(x, dx) + flip(c, dc)
            for xb in (0, 1):
                d_out[n, xb] = dpart[xb, aligned(theirs * 64, 64), :].astype(BF16)
            d_copy(n).start()

    def decoder_middle():
        for n in range(3):
            d_copy(n).wait_recv()
        for xb in (0, 1):
            part = dpart[xb, aligned(shard * 64, 64), :]
            for n in range(3):
                part = part + d_in[n, xb].astype(F32)
            f_out[xb] = part.astype(BF16)

            @pl.when(final_to(xb) != dp)
            def _():
                f_copy(xb).start()

            @pl.when(final_to(xb) == dp)
            def _():
                f_in[p] = f_out[xb]

    def decoder_end():
        for n in (0, 1):

            @pl.when(final_from(n) != dp)
            def _():
                f_wait(n)

        gdec_o[...] = f_in[0].astype(F32) + f_in[1].astype(F32)

    for part in range(SPLIT):
        h_wait(STEPS - 1, part)
        decode(STEPS - 1, part)
        backward(STEPS - 1, part)
    decoder_start()
    extras(STEPS - 1)
    dg_out = [pltpu.make_async_copy(dg.at[t], dg_o.at[t], out_sem.at[1 + t]) for t in range(STEPS)]
    dg_out[STEPS - 1].start()
    for t in reversed(range(STEPS - 1)):
        for part in range(SPLIT):
            backward(t, part)
        dg_out[t].start()
        if t == STEPS - 2:
            decoder_middle()
        extras(t)
    decoder_end()

    for xb in (0, 1):
        dc0_o[:, pl.ds(xb * ROWS, ROWS)] = dcn[xb]
    at_row = lax.broadcasted_iota(jnp.int32, (288, 128), 0)
    at_col = lax.broadcasted_iota(jnp.int32, (288, 128), 1)
    block = jnp.where((at_row < 275) & (at_col < INPUTS), emb[pl.ds(0, 288), :], 0.0)
    for n in range(3):
        block = jnp.where(at_row == 276 + n, totals["bias"][:, n * 128 : n * 128 + 128], block)
    block = jnp.where((at_row == 279) & (at_col == 0), totals["loss"], block)
    emb_o[...] = block

    for q in range(SLICES):
        for target in (0, 1):

            @pl.when(c + 2 * target != z)
            def _():
                z_copy(target, q).wait_send()

        for n in (0, 1):
            x_copy(gates[n], q).wait_send()
            c_copy(gates[n], q, n, False).wait_send()
            c_copy(gates[n], q, n, True).wait_send()
    for n in range(5):
        for d in (1, 2):
            group_copy(d, n).wait_send()
        if n < 3:
            corner_copy(n).wait_send()
        else:
            group_copy(3, n).wait_send()
    for n in range(3):
        d_copy(n).wait_send()
    for xb in (0, 1):

        @pl.when(final_to(xb) != dp)
        def _():
            f_copy(xb).wait_send()

    far_copy().wait_send()
    over_copy().wait_send()
    for xs in (0, 1):
        twin_copy(xs).wait_send()
    for t in range(STEPS):
        for part in range(SPLIT):
            for d in (1, 2, 3):
                for xb in (0, 1):
                    h_copy(t, part, xb, d).wait_send()
                if t > 0:
                    b_copy(t, part, d).wait_send()
    hx_out.wait()
    for t in range(STEPS):
        dg_out[t].wait()


def sum_kernel(
    dg,
    hx,
    dh0,
    dc0,
    emb,
    gdec_own,
    grad_o,
    emb_o,
    norm_o,
    gh_o,
    gc_o,
    c_out,
    c_in,
    kept,
    x_out,
    x_in,
    z_out,
    z_in,
    gh_out,
    gh_in,
    gc_out,
    gc_in,
    e_in,
    n_out,
    n_in,
    c_send,
    c_recv,
    x_send,
    x_recv,
    z_send,
    z_recv,
    g_send,
    g_recv,
    e_send,
    e_recv,
    n_send,
    n_recv,
):
    s = spots()
    z, y, x, c, k, zi, p = s["z"], s["y"], s["x"], s["c"], s["k"], s["zi"], s["p"]
    dp, shard = s["dp"], s["shard"]
    across = device(s, x=1 - x)
    twin = device(s, c=1 - c)
    far = device(s, z=2 * (1 - p) + zi)
    peers = {d: peer(s, d) for d in (1, 2, 3)}
    core = z % 2
    column = [(dz, dc) for dz in range(4) for dc in range(2) if (dz, dc) != (0, 0)]
    plane = [(dy, dx) for dy in range(2) for dx in range(2) if (dy, dx) != (0, 0)]

    def flip(value, by):
        return 1 - value if by else value

    def column_to(dz, dc):
        return device(s, z=(z + dz) % 4, c=flip(c, dc))

    def column_from(dz, dc):
        return device(s, z=(z + 4 - dz) % 4, c=flip(c, dc))

    def plane_to(dy, dx):
        return device(s, y=flip(y, dy), x=flip(x, dx))

    for dz, dc in column:
        signal(column_from(dz, dc))
    for dy, dx in plane:
        signal(plane_to(dy, dx))
    signal(peers[3]["dev"])
    pl.semaphore_wait(pltpu.get_barrier_semaphore(), 11)

    def state_copies(d, sender=True):
        there = peers[d]
        rows = aligned(there["k"] * 64, 64)
        result = [
            remote(gh_out.at[d - 1], gh_in.at[d - 1], g_send.at[d - 1, 0], g_recv.at[d - 1, 0], there["dev"]),
            remote(gc_out.at[d - 1], gc_in.at[d - 1], g_send.at[d - 1, 1], g_recv.at[d - 1, 1], there["dev"]),
        ]
        return result

    def early():
        for d in (3, 1, 2):
            rows = aligned(peers[d]["k"] * 64, 64)
            gh_out[d - 1] = dh0[rows, :].astype(BF16)
            gc_out[d - 1] = dc0[rows, :].astype(BF16)
            for copy in state_copies(d):
                copy.start()

    tiles = ((0, 512), (512, 512), (1024, 512), (1536, 640))

    def block_of(b, store):
        for start, size in tiles:
            at = pl.ds(start, size)
            store(at, dot_tn(dg[:, cols(b)], hx[:, at]))

    def c_copy(n, q):
        rows = pl.ds(q * SLICE, SLICE)
        return remote(c_out.at[n, rows], c_in.at[n, rows], c_send.at[n, q], c_recv.at[n, q], twin)

    def x_copy(i, q):
        rows = pl.ds(q * SLICE, SLICE)
        return remote(x_out.at[i, rows], x_in.at[i, rows], x_send.at[i, q], x_recv.at[i, q], across)

    def z_copy(i, q):
        rows = pl.ds(q * SLICE, SLICE)
        return remote(
            z_out.at[i, rows],
            z_in.at[p, rows],
            z_send.at[i, q],
            z_recv.at[p, q],
            device(s, z=c + 2 * gates[i], c=core),
        )

    def z_wait(n, q):
        rows = pl.ds(q * SLICE, SLICE)
        remote(z_out.at[n, rows], z_in.at[n, rows], z_send.at[n, q], z_recv.at[n, q], across).wait_recv()

    def for_twin(n, b):
        def store(at, value):
            c_out[n, :, at] = value.astype(BF16)

        block_of(b, store)
        for q in range(SLICES):
            c_copy(n, q).start()

    def keep(i, b):
        def store(at, value):
            kept[i, :, at] = value

        block_of(b, store)

    def add_twin(i, n, q):
        rows = pl.ds(q * SLICE, SLICE)
        c_copy(n, q).wait_recv()
        return kept[i, rows] + c_in[n, rows].astype(F32)

    half = aligned(c * 144, 144)
    rest = aligned((1 - c) * 144, 144)
    hops = (twin, across, far, peers[2]["dev"], peers[1]["dev"], twin)

    def e_copy(n):
        if n == 0:
            return remote(emb_o.at[rest], e_in.at[0], e_send.at[0], e_recv.at[0], hops[0])
        if n == 5:
            return remote(emb_o.at[half], e_in.at[5], e_send.at[5], e_recv.at[5], hops[5])
        return remote(e_out_of(n), e_in.at[n], e_send.at[n], e_recv.at[n], hops[n])

    def e_out_of(n):
        return e_in.at[5 + n]

    def e_start(n):
        if n in (1, 2, 3, 4):
            e_in[5 + n] = emb_o[half, :]
        e_copy(n).start()

    def e_finish(n):
        if n == 5:
            e_copy(5).wait()
            emb_o[rest, :] = e_in[5]
            return
        e_copy(n).wait()
        emb_o[half, :] = emb_o[half, :] + e_in[n]

    gates = (1 - p, p)

    def pass_on(n, q):
        i = gates[n]
        rows = pl.ds(q * SLICE, SLICE)
        x_copy(n, q).wait_recv()
        total = add_twin(n, 2 + n, q) + x_in[n, rows].astype(F32)
        z_out[n, rows] = total.astype(BF16)

        @pl.when(c + 2 * i != z)
        def _():
            z_copy(n, q).start()

        @pl.when(c + 2 * i == z)
        def _():
            z_in[p, rows] = z_out[n, rows]

    def to_across(n):
        for q in range(SLICES):
            x_out[n, pl.ds(q * SLICE, SLICE)] = add_twin(2, n, q).astype(BF16)
            x_copy(n, q).start()

    emb_o[...] = emb[...]
    e_start(0)
    for_twin(0, 2 * (1 - c + 2 * gates[0]) + 1 - x)
    e_finish(0)
    e_start(1)
    keep(2, 2 * (c + 2 * gates[0]) + 1 - x)
    to_across(0)
    e_finish(1)
    e_start(2)
    for_twin(2, 2 * (1 - c + 2 * gates[0]) + x)
    keep(0, 2 * (c + 2 * gates[0]) + x)
    e_finish(2)
    e_start(3)
    for_twin(1, 2 * (1 - c + 2 * gates[1]) + 1 - x)
    keep(2, 2 * (c + 2 * gates[1]) + 1 - x)
    e_finish(3)
    e_start(4)
    for q in range(SLICES):
        pass_on(0, q)
        if q == 0:
            to_across(1)
            early()
        if q == 1:
            for_twin(3, 2 * (1 - c + 2 * gates[1]) + x)
        if q == 2:
            keep(1, 2 * (c + 2 * gates[1]) + x)
        if q == 3:
            e_finish(4)
            e_start(5)
    for q in range(SLICES):
        pass_on(1, q)
    e_finish(5)

    squares = jnp.zeros((1, 1), F32)

    def square_sum(value):
        return jnp.sum(jnp.sum(value * value, axis=1, keepdims=True), axis=0, keepdims=True)

    squares = squares + square_sum(gdec_own[...])
    for q in range(SLICES):
        rows = pl.ds(q * SLICE, SLICE)
        for n in (0, 1):

            @pl.when(jnp.logical_or(core != c, p != n))
            def _():
                z_wait(n, q)

        final = z_in[0, rows].astype(F32) + z_in[1, rows].astype(F32)
        grad_o[rows, :] = final
        squares = squares + square_sum(final)

    def n_copy(n):
        if n < 7:
            return remote(n_out.at[0], n_in.at[n], n_send.at[n], n_recv.at[n], column_to(*column[n]))
        return remote(n_out.at[1], n_in.at[n], n_send.at[n], n_recv.at[n], plane_to(*plane[n - 7]))

    n_out[0] = jnp.broadcast_to(squares, (8, 128))
    for n in range(7):
        n_copy(n).start()
    own = aligned(k * 64, 64)
    total = dh0[own, :]
    for d in (1, 2, 3):
        for copy in state_copies(d):
            copy.wait_recv()
        total = total + gh_in[d - 1].astype(F32)
    gh_o[...] = total
    for xb in (0, 1):
        gc_o[:, cols(stripe(y, zi, xb))] = dc0[own, pl.ds(xb * ROWS, ROWS)]
        for d in (1, 2, 3):
            there = peers[d]
            gc_o[:, cols(stripe(there["y"], there["zi"], xb))] = gc_in[d - 1, :, pl.ds(xb * ROWS, ROWS)].astype(F32)
    total = n_out[0]
    for n in range(7):
        n_copy(n).wait_recv()
        total = total + n_in[n]
    n_out[1] = total
    for n in range(7, 10):
        n_copy(n).start()
    at_row = lax.broadcasted_iota(jnp.int32, (288, 128), 0)
    shared = square_sum(jnp.where(at_row == 279, 0.0, emb_o[...]))
    for n in range(7, 10):
        n_copy(n).wait_recv()
        total = total + n_in[n]
    norm_o[...] = total + shared

    for n in range(4):
        for q in range(SLICES):
            c_copy(n, q).wait_send()
    for i in (0, 1):
        for q in range(SLICES):
            x_copy(i, q).wait_send()

            @pl.when(c + 2 * gates[i] != z)
            def _():
                z_copy(i, q).wait_send()

    for d in (1, 2, 3):
        for copy in state_copies(d):
            copy.wait_send()
    for n in range(10):
        n_copy(n).wait_send()


def split_local(
    char_ids,
    targets,
    hidden_start,
    cell_start,
    embedding,
    input_weight,
    hidden_weight,
    gate_bias,
    decoder_weight,
    decoder_bias,
    momentum_embed,
    momentum_input,
    momentum_hidden,
    momentum_gate,
    momentum_decoder,
    momentum_outbias,
):
    streams = char_ids.shape[0]
    vocab = embedding.shape[0]
    shape = jax.ShapeDtypeStruct
    wext = jnp.concatenate(
        [
            hidden_weight.astype(BF16),
            input_weight.astype(BF16),
            gate_bias.astype(BF16)[:, None],
            jnp.zeros((ROWS, WIDE - HID - INPUTS - 1), BF16),
        ],
        axis=1,
    )
    meta = jnp.pad(jnp.concatenate([char_ids, targets], axis=1), ((0, 0), (0, 120)))
    wout = jnp.pad(decoder_weight.astype(BF16), ((0, 0), (0, CHARS - vocab)))
    table = jnp.concatenate(
        [embedding.astype(BF16), jnp.ones((vocab, 1), BF16), jnp.zeros((vocab, WIDE - HID - INPUTS - 1), BF16)],
        axis=1,
    )
    table = jnp.pad(table, ((0, CHARS - vocab), (0, 0)))
    dbias = jnp.broadcast_to(
        jnp.pad(decoder_bias, (0, CHARS - vocab), constant_values=-1e30)[None, :], (8, CHARS)
    )
    vm = pl.BlockSpec(memory_space=pltpu.VMEM)
    hbm = pl.BlockSpec(memory_space=pl.ANY)
    dma = pltpu.SemaphoreType.DMA
    hx, dg, dh0, dc0, emb, gdec_own = pl.pallas_call(
        step_kernel,
        out_shape=(
            shape((STEPS, ROWS, WIDE), BF16),
            shape((STEPS, ROWS, HID), BF16),
            shape((ROWS, HID), F32),
            shape((ROWS, 512), F32),
            shape((288, 128), F32),
            shape((64, CHARS), F32),
        ),
        in_specs=[vm] * 7,
        out_specs=(hbm, hbm, vm, vm, vm, vm),
        scratch_shapes=[
            pltpu.VMEM((HID, WIDE), BF16),
            pltpu.VMEM((8, WIDE, ROWS), BF16),
            pltpu.VMEM((STEPS + 1, ROWS, WIDE), BF16),
            pltpu.VMEM((STEPS, 8, ROWS, ROWS), F32),
            pltpu.VMEM((STEPS + 1, 2, ROWS, ROWS), F32),
            pltpu.VMEM((STEPS, ROWS, HID), BF16),
            pltpu.VMEM((STEPS - 1, 3, ROWS, 512), BF16),
            pltpu.VMEM((STEPS - 1, 3, ROWS, 512), BF16),
            pltpu.VMEM((ROWS, 512), F32),
            pltpu.VMEM((2, ROWS, ROWS), F32),
            pltpu.VMEM((8, 4, 64, CHARS), BF16),
            pltpu.VMEM((STEPS, ROWS, CHARS), BF16),
            pltpu.VMEM((ROWS, 128), jnp.int32),
            pltpu.VMEM((CHARS, 128), F32),
            pltpu.VMEM((2, ROWS, ROWS), BF16),
            pltpu.VMEM((2, ROWS, CHARS), F32),
            pltpu.VMEM((3, 2, 64, CHARS), BF16),
            pltpu.VMEM((3, 2, 64, CHARS), BF16),
            pltpu.VMEM((2, 64, CHARS), BF16),
            pltpu.VMEM((2, 64, CHARS), BF16),
            dma((3, 5)),
            dma((3, 5)),
            dma((2, SLICES)),
            dma((2, SLICES)),
            dma((2, SLICES)),
            dma((2, SLICES)),
            dma((2, 2, SLICES)),
            dma((2, 2, SLICES)),
            dma((4,)),
            dma((4,)),
            dma((STEPS, SPLIT, 2, 3)),
            dma((STEPS, SPLIT, 2, 3)),
            dma((STEPS - 1, SPLIT, 3)),
            dma((STEPS - 1, SPLIT, 3)),
            dma((3,)),
            dma((3,)),
            dma((2,)),
            dma((2,)),
            dma((1 + STEPS,)),
        ],
        compiler_params=pltpu.CompilerParams(
            collective_id=0, has_side_effects=True, vmem_limit_bytes=60 * 2**20
        ),
    )(wext, hidden_start.astype(BF16), cell_start.astype(BF16), meta, wout, table, dbias)
    grad, emb, norm, grad_hidden_start, grad_cell_start = pl.pallas_call(
        sum_kernel,
        out_shape=(
            shape((ROWS, WIDE), F32),
            shape((288, 128), F32),
            shape((8, 128), F32),
            shape((64, HID), F32),
            shape((64, HID), F32),
        ),
        in_specs=[vm] * 6,
        out_specs=(vm,) * 5,
        scratch_shapes=[
            pltpu.VMEM((4, ROWS, WIDE), BF16),
            pltpu.VMEM((4, ROWS, WIDE), BF16),
            pltpu.VMEM((3, ROWS, WIDE), F32),
            pltpu.VMEM((2, ROWS, WIDE), BF16),
            pltpu.VMEM((2, ROWS, WIDE), BF16),
            pltpu.VMEM((2, ROWS, WIDE), BF16),
            pltpu.VMEM((2, ROWS, WIDE), BF16),
            pltpu.VMEM((3, 64, HID), BF16),
            pltpu.VMEM((3, 64, HID), BF16),
            pltpu.VMEM((3, 64, 512), BF16),
            pltpu.VMEM((3, 64, 512), BF16),
            pltpu.VMEM((10, 144, 128), F32),
            pltpu.VMEM((2, 8, 128), F32),
            pltpu.VMEM((10, 8, 128), F32),
            dma((4, SLICES)),
            dma((4, SLICES)),
            dma((2, SLICES)),
            dma((2, SLICES)),
            dma((2, SLICES)),
            dma((2, SLICES)),
            dma((3, 2)),
            dma((3, 2)),
            dma((6,)),
            dma((6,)),
            dma((10,)),
            dma((10,)),
        ],
        compiler_params=pltpu.CompilerParams(
            collective_id=1, has_side_effects=True, vmem_limit_bytes=60 * 2**20
        ),
    )(dg.reshape(STEPS * ROWS, HID), hx.reshape(STEPS * ROWS, WIDE), dh0, dc0, emb, gdec_own)
    grad_norm = jnp.sqrt(norm[0:1, 0])
    factor = CLIP / jnp.maximum(grad_norm[0], CLIP)
    streams_all = streams * lax.axis_size("dp") * lax.axis_size("shard")
    loss = emb[279, 0:1] / streams_all
    grads = (
        emb[:vocab, :INPUTS],
        grad[:, HID : HID + INPUTS],
        grad[:, :HID],
        grad[:, HID + INPUTS],
        gdec_own[:, :vocab],
        emb[276:279].reshape(-1)[:vocab],
    )
    momenta = (
        momentum_embed,
        momentum_input,
        momentum_hidden,
        momentum_gate,
        momentum_decoder,
        momentum_outbias,
    )
    updated = tuple(MOMENTUM * momenta[n] + factor * grads[n] for n in range(6))
    return (loss, grad_norm, grad_hidden_start, grad_cell_start) + grads + updated


def solution(mesh):
    fits = mesh.shape["dp"] == 8 and mesh.shape["shard"] == 4
    placed = (
        P(("dp", "shard"), None),
        P(("dp", "shard"), None),
        P(("dp", "shard"), None),
        P(("dp", "shard"), None),
        P(),
        P(("dp", "shard"), None),
        P(("dp", "shard"), None),
        P(("dp", "shard")),
        P(("dp", "shard"), None),
        P(),
        P(),
        P(("dp", "shard"), None),
        P(("dp", "shard"), None),
        P(("dp", "shard")),
        P(("dp", "shard"), None),
        P(),
    )
    return jax.shard_map(
        split_local if fits else local,
        mesh=mesh,
        in_specs=placed,
        out_specs=(
            P(),
            P(),
            P(("dp", "shard"), None),
            P(("dp", "shard"), None),
            P(),
            P(("dp", "shard"), None),
            P(("dp", "shard"), None),
            P(("dp", "shard")),
            P(("dp", "shard"), None),
            P(),
            P(),
            P(("dp", "shard"), None),
            P(("dp", "shard"), None),
            P(("dp", "shard")),
            P(("dp", "shard"), None),
            P(),
        ),
        check_vma=False,
    )
```

profile of v0, /device:TPU:0, one launch (start us, length us, event | category | flops | bytes accessed | tf_op | source)
XLA Modules:
  0.0 284.8 jit_solution(7304339670585709567)
XLA Ops:
  0.6 0.0 copy-start.9
  0.7 0.0 copy-start.19
  0.7 1.8 convert_element_type.25
  2.4 0.0 copy-done.9
  2.4 0.0 copy-start.1
  2.5 0.0 copy-start.2
  2.5 0.0 copy-start.8
  2.5 0.1 copy.51
  2.6 0.0 copy-done.19
  2.6 0.1 broadcast_in_dim.23
  2.8 0.0 copy-start.11
  2.8 0.0 copy-start.16
  2.8 0.0 copy-start.17
  2.8 0.0 copy-start.15
  2.8 1.9 concatenate.9.wext
  4.7 0.0 copy-done.1
  4.7 0.7 convert_element_type.28.h_own
  5.5 0.0 copy-done.2
  5.5 0.7 convert_element_type.29.cell_own
  6.2 0.0 copy-done.8
  6.2 0.1 pad.22.clone
  6.3 0.1 pad.21.clone
  6.4 0.7 pad.18.table
  7.1 0.0 copy-done.11
  7.1 0.6 pad.17.wout_own
  7.7 0.0 copy-done.16
  7.7 0.0 copy-done.17
  7.7 0.1 copy.53
  7.8 0.6 pad.16.meta_own
  8.4 0.0 copy-done.15
  8.4 0.6 broadcast_in_dim.22.dbias
  9.0 172.3 %shard_map.279 = (bf16[4,256,2176]{2,1,0:T(8,128)(2,1)}, bf16[4,256,2048]{2,1,0:T(8,128)(2,1)}, f32[256,2048]{1,0:T(8,128)}, f32[256,512]{1,0:T(8,128)}, f32[288,128]{1,0:T(8,128)}, /*index=5*/f32[64,384]{1,0:T(8,128)}) custom-call(bf16[256,2176]{1,0:T(8,128)(2,1)} %concatenate.9.wext, bf16[64,2048]{1,0:T(8,128)(2,1)} %convert_element_type.28.h_own, ...), custom_call_target="tpu_custom_call" | custom-call | tf_op jit(solution)/shard_map/pallas_call | solution.py:1214
  181.3 0.0 copy-start.18
  181.3 0.0 copy-start.14
  181.4 0.0 copy-start
  181.4 85.1 %shard_map.280 = (f32[256,2176]{1,0:T(8,128)}, f32[288,128]{1,0:T(8,128)}, f32[8,128]{1,0:T(8,128)}, f32[64,2048]{1,0:T(8,128)}, f32[64,2048]{1,0:T(8,128)}) custom-call(bf16[1024,2048]{1,0:T(8,128)(2,1)} %bitcast.9, bf16[1024,2176]{1,0:T(8,128)(2,1)} %bitcast.8, f32[256,2048]{1,0:T(8,128)} %get-tuple-element.29.dh0, f32[256,512]{1,0:T(8,128)} %get-tuple-element.30.dc0, ...), custom_call_target="tpu_custom_call" | custom-call | tf_op jit(solution)/shard_map/pallas_call | solution.py:1271
  266.4 1.2 slice.28
  268.4 1.1 slice_reduce_fusion
  269.4 0.0 copy-done.18
  269.5 0.0 copy-start.13
  269.5 0.6 multiply_add_fusion.5
  270.0 0.7 slice_bitcast_fusion
  270.7 0.0 copy-done.14
  270.7 0.6 multiply_add_fusion.4
  271.3 0.0 copy-done
  271.3 0.0 copy-start.7
  271.3 0.0 copy-start.5
  271.3 0.0 copy-start.12
  271.3 4.2 %multiply_add_fusion = (f32[256,2048]{1,0:T(8,128)}, f32[256,2048]{1,0:T(8,128)}) fusion(f32[256,2048]{1,0:T(8,128)S(1)} %copy-done, f32[]{:T(128)} %bitcast.5, f32[256,2176]{1,0:T(8,128)} %get-tuple-element.37), kind=kLoop, calls=%fused_computation | loop fusion | flops 1572864 | bytes 8388612 | tf_op jit(solution)/shard_map/add | solution.py:1334
  275.5 0.0 copy-done.13
  275.5 0.0 copy-done.10
  275.5 0.1 copy.54
  275.6 1.0 multiply_add_fusion.2
  276.6 0.7 copy.55
  277.4 0.7 copy.56
  278.1 0.0 copy-done.6
  278.1 0.0 copy-done.7
  278.1 0.7 multiply_add_fusion.1
  278.8 0.0 copy-done.5
  278.9 0.0 copy-done.12
  278.9 0.7 multiply_add_fusion.3
  279.6 0.5 slice.27
  280.7 0.8 copy.59
  281.5 0.8 copy.60
  (15 shorter events, 0.1 us)
Async XLA Ops:
  0.6 1.8 copy-start.9
  0.7 2.0 copy-start.19
  2.4 2.3 copy-start.1
  2.5 3.0 %copy-start.2 = (f32[64,2048]{1,0:T(8,128)S(1)}, f32[64,2048]{1,0:T(8,128)}, u32[]{:S(2)}) copy-start(f32[64,2048]{1,0:T(8,128)} %param.19) | copy-start | bytes 1572868
  2.5 3.7 %copy-start.8 = (f32[275,100]{1,0:T(8,128)S(1)}, f32[275,100]{1,0:T(8,128)}, u32[]{:S(2)}) copy-start(f32[275,100]{1,0:T(8,128)} %param.20) | copy-start | bytes 330004
  2.8 4.3 %copy-start.11 = (f32[64,275]{1,0:T(8,128)S(1)}, f32[64,275]{1,0:T(8,128)}, u32[]{:S(2)}) copy-start(f32[64,275]{1,0:T(8,128)} %param.24) | copy-start | bytes 211204
  2.8 4.9 %copy-start.16 = (s32[64,4]{0,1:T(4,128)S(1)}, s32[64,4]{0,1:T(4,128)}, u32[]{:S(2)}) copy-start(s32[64,4]{0,1:T(4,128)} %param.17) | copy-start | bytes 3076
  2.8 4.9 %copy-start.17 = (s32[64,4]{0,1:T(4,128)S(1)}, s32[64,4]{0,1:T(4,128)}, u32[]{:S(2)}) copy-start(s32[64,4]{0,1:T(4,128)} %param.16) | copy-start | bytes 3076
  2.8 5.6 %copy-start.15 = (f32[275]{0:T(512)S(1)}, f32[275]{0:T(512)}, u32[]{:S(2)}) copy-start(f32[275]{0:T(512)} %param.25) | copy-start | bytes 3304
  181.3 88.1 %copy-start.18 = (f32[256]{0:T(256)S(1)}, f32[256]{0:T(256)}, u32[]{:S(2)}) copy-start(f32[256]{0:T(256)} %param.29) | copy-start | bytes 3076
  181.3 89.4 %copy-start.14 = (f32[275]{0:T(512)S(1)}, f32[275]{0:T(512)}, u32[]{:S(2)}) copy-start(f32[275]{0:T(512)} %param.31) | copy-start | bytes 3304
  181.4 89.9 %copy-start = (f32[256,2048]{1,0:T(8,128)S(1)}, f32[256,2048]{1,0:T(8,128)}, u32[]{:S(2)}) copy-start(f32[256,2048]{1,0:T(8,128)} %param.28) | copy-start | bytes 6291460
  269.5 6.1 %copy-start.13 = (f32[256]{0:T(256)}, f32[256]{0:T(256)S(1)}, u32[]{:S(2)}) copy-start(f32[256]{0:T(256)S(1)} %slice_reduce_fusion) | copy-start | bytes 3076
  271.3 4.2 %copy-start.10 = (f32[256,100]{0,1:T(8,128)S(1)}, f32[256,100]{0,1:T(8,128)}, u32[]{:S(2)}) copy-start(f32[256,100]{0,1:T(8,128)} %param.27) | copy-start | bytes 307204
  271.3 6.8 %copy-start.6 = (f32[288,128]{1,0:T(8,128)S(1)}, f32[288,128]{1,0:T(8,128)}, u32[]{:S(2)}) copy-start(f32[288,128]{1,0:T(8,128)} %get-tuple-element.33) | copy-start | bytes 442372
  271.3 6.8 %copy-start.7 = (f32[275,100]{1,0:T(8,128)S(1)}, f32[275,100]{1,0:T(8,128)}, u32[]{:S(2)}) copy-start(f32[275,100]{1,0:T(8,128)} %param.26) | copy-start | bytes 330004
  271.3 7.5 %copy-start.5 = (f32[64,384]{1,0:T(8,128)S(1)}, f32[64,384]{1,0:T(8,128)}, u32[]{:S(2)}) copy-start(f32[64,384]{1,0:T(8,128)} %get-tuple-element.32.gdec_own) | copy-start | bytes 294916
  271.3 7.5 %copy-start.12 = (f32[64,275]{1,0:T(8,128)S(1)}, f32[64,275]{1,0:T(8,128)}, u32[]{:S(2)}) copy-start(f32[64,275]{1,0:T(8,128)} %param.30) | copy-start | bytes 211204
  275.5 5.2 %copy-start.4 = (f32[64,2048]{1,0:T(8,128)S(1)}, f32[64,2048]{1,0:T(8,128)}, u32[]{:S(2)}) copy-start(f32[64,2048]{1,0:T(8,128)} %get-tuple-element.130) | copy-start | bytes 1572868
  275.5 6.0 %copy-start.3 = (f32[64,2048]{1,0:T(8,128)S(1)}, f32[64,2048]{1,0:T(8,128)}, u32[]{:S(2)}) copy-start(f32[64,2048]{1,0:T(8,128)} %get-tuple-element.131) | copy-start | bytes 1572868
where the time goes:
time: 288 us; the launch traced here: 285 us
  Pallas kernels  257 us (89%)
  local copies, waits for them, and re-layouts  11.6 us (4%)
  other arithmetic  11 us (4%)
  between operations  4.79 us (2%)
    pallas_call x1, Pallas kernels, split_local(): pl.pallas_call(step_kernel, out_shape=(shape((STEPS, ROWS, WIDE), BF16),...  172 us
    pallas_call x1, Pallas kernels, split_local(): pl.pallas_call(sum_kernel, out_shape=(shape((ROWS, WIDE), F32), shape((28...  85.1 us
    add x6, other arithmetic, split_local(): MOMENTUM * momenta[n] + factor * grads[n]  7.74 us

commit v1 on v0

--- a/solution.py
+++ b/solution.py
@@ -353,13 +353,16 @@
 
 
 def step_kernel(
-    wext,
-    h_own,
-    cell_own,
-    meta_own,
-    wout_own,
-    table,
-    dbias,
+    ids_in,
+    targets_in,
+    hidden_in,
+    cell_in,
+    embedding_in,
+    input_in,
+    weight_in,
+    gate_in,
+    decoder_in,
+    outbias_in,
     hx_o,
     dg_o,
     dh0_o,
@@ -386,6 +389,15 @@
     d_in,
     f_out,
     f_in,
+    wext,
+    h_own,
+    cell_own,
+    meta_own,
+    wout_own,
+    table,
+    dbias,
+    narrow,
+    ids_wide,
     g_send,
     g_recv,
     wz_send,
@@ -451,6 +463,21 @@
             signal((final_from(n), shard))
 
         away = away + jnp.where(final_to(n) != dp, 1, 0)
+
+    narrow[...] = jnp.zeros_like(narrow)
+    narrow[pl.ds(0, INPUTS), :] = input_in[...]
+    narrow[pl.ds(INPUTS, 1), :] = gate_in[...]
+    wext[:, pl.ds(HID, WIDE - HID)] = narrow[...].T.astype(BF16)
+    wext[:, pl.ds(0, HID)] = weight_in[...].astype(BF16)
+    ids_wide[...] = jnp.zeros_like(ids_wide)
+    ids_wide[pl.ds(0, STEPS), pl.ds(0, 64)] = ids_in[...]
+    ids_wide[pl.ds(STEPS, STEPS), pl.ds(0, 64)] = targets_in[...]
+    meta_own[...] = ids_wide[...].T[0:64, :]
+    h_own[...] = hidden_in[...].astype(BF16)
+    vocab = decoder_in.shape[1]
+    wout_own[...] = jnp.zeros_like(wout_own)
+    wout_own[:, pl.ds(0, vocab)] = decoder_in[...].astype(BF16)
+    cell_own[...] = cell_in[...].astype(BF16)
     pl.semaphore_wait(pltpu.get_barrier_semaphore(), 7 + 2 * off_core + away)
 
     def z_copy(target, q):
@@ -543,6 +570,11 @@
     for xb in (0, 1):
         cells[xb, own] = cell_own[:, cols(mine[xb])]
 
+    dbias[...] = jnp.full(dbias.shape, -1e30, F32)
+    dbias[pl.ds(0, 1), pl.ds(0, vocab)] = outbias_in[...]
+    table[...] = jnp.where(lax.broadcasted_iota(jnp.int32, table.shape, 1) == INPUTS, 1.0, 0.0)
+    table[pl.ds(0, vocab), pl.ds(0, INPUTS)] = embedding_in[...].astype(BF16).astype(F32)
+
     def group_wait(d, n):
         there = peers[d]
         rows = aligned(there["k"] * 64, 64)
@@ -559,6 +591,11 @@
 
     lanes = lax.broadcasted_iota(jnp.int32, (ROWS, CHARS), 1)
 
+    def embed_inputs():
+        for t in range(STEPS):
+            one = jnp.where(metas[:, t : t + 1] == lanes, 1.0, 0.0).astype(BF16)
+            hx[t, :, pl.ds(HID, WIDE - HID)] = dot(one, table[...].astype(BF16)).astype(BF16)
+
     def turn(b):
         wt[b] = w2[cols(b), :].T
 
@@ -583,6 +620,10 @@
                 corner_copy(m).start()
         if n == 1 and q < 2:
             turn(2 * (c + 2 * p) + q)
+        if n == 1 and q == 3:
+            group_wait(1, 0)
+            corner_copy(0, False).wait_recv()
+            embed_inputs()
         if n == 1 and q == 2:
             for other in (False, True):
                 for slot in range(SLICES):
@@ -598,16 +639,13 @@
             c_copy(1 - p, q, 1, other, False).wait_recv()
     for xs in (0, 1):
         turn(2 * (1 - c + 2 * (1 - p)) + xs)
-    for n in (0, 1, 2):
+    for n in (1, 2):
         group_wait(1, n)
         corner_copy(n, False).wait_recv()
     for n in (3, 4):
         for d in (1, 2, 3):
             group_wait(d, n)
         call[0, n - 3] = cells[n - 3].astype(F32)
-    for t in range(STEPS):
-        one = jnp.where(metas[:, t : t + 1] == lanes, 1.0, 0.0).astype(BF16)
-        hx[t, :, pl.ds(HID, WIDE - HID)] = dot(one, table[...]).astype(BF16)
 
     def far_copy(sender=True):
         first = 4 * p if sender else 4 * (1 - p)
@@ -1168,6 +1206,59 @@
         n_copy(n).wait_send()
 
 
+def finish_kernel(
+    streams_all,
+    grad,
+    emb,
+    squares,
+    gdec,
+    gh,
+    gc,
+    m_embed,
+    m_input,
+    m_hidden,
+    m_gate,
+    m_decoder,
+    m_outbias,
+    loss_o,
+    norm_o,
+    gh_o,
+    gc_o,
+    g_embed,
+    g_input,
+    g_hidden,
+    g_gate,
+    g_decoder,
+    g_outbias,
+    n_embed,
+    n_input,
+    n_hidden,
+    n_gate,
+    n_decoder,
+    n_outbias,
+):
+    norm = jnp.sqrt(squares[0:1, 0:1])
+    norm_o[0] = norm[0, 0]
+    factor = CLIP / jnp.maximum(norm, CLIP)
+    loss_o[0] = emb[279, 0] / streams_all
+    gh_o[...] = gh[...]
+    gc_o[...] = gc[...]
+
+    def out(value, momentum, grad_ref, new_ref):
+        grad_ref[...] = value
+        new_ref[...] = MOMENTUM * momentum[...] + factor * value
+
+    vocab = m_outbias.shape[1]
+    out(emb[pl.ds(0, vocab), pl.ds(0, INPUTS)], m_embed, g_embed, n_embed)
+    turned = grad[:, pl.ds(HID, WIDE - HID)].T
+    out(turned[0:INPUTS, :], m_input, g_input, n_input)
+    out(turned[INPUTS : INPUTS + 1, :], m_gate, g_gate, n_gate)
+    out(grad[:, pl.ds(0, HID)], m_hidden, g_hidden, n_hidden)
+    out(gdec[:, pl.ds(0, vocab)], m_decoder, g_decoder, n_decoder)
+    row = jnp.concatenate([emb[276 + n : 277 + n, :] for n in range(3)], axis=1)
+    out(row[:, 0:vocab], m_outbias, g_outbias, n_outbias)
+
+
 def split_local(
     char_ids,
     targets,
@@ -1189,25 +1280,6 @@
     streams = char_ids.shape[0]
     vocab = embedding.shape[0]
     shape = jax.ShapeDtypeStruct
-    wext = jnp.concatenate(
-        [
-            hidden_weight.astype(BF16),
-            input_weight.astype(BF16),
-            gate_bias.astype(BF16)[:, None],
-            jnp.zeros((ROWS, WIDE - HID - INPUTS - 1), BF16),
-        ],
-        axis=1,
-    )
-    meta = jnp.pad(jnp.concatenate([char_ids, targets], axis=1), ((0, 0), (0, 120)))
-    wout = jnp.pad(decoder_weight.astype(BF16), ((0, 0), (0, CHARS - vocab)))
-    table = jnp.concatenate(
-        [embedding.astype(BF16), jnp.ones((vocab, 1), BF16), jnp.zeros((vocab, WIDE - HID - INPUTS - 1), BF16)],
-        axis=1,
-    )
-    table = jnp.pad(table, ((0, CHARS - vocab), (0, 0)))
-    dbias = jnp.broadcast_to(
-        jnp.pad(decoder_bias, (0, CHARS - vocab), constant_values=-1e30)[None, :], (8, CHARS)
-    )
     vm = pl.BlockSpec(memory_space=pltpu.VMEM)
     hbm = pl.BlockSpec(memory_space=pl.ANY)
     dma = pltpu.SemaphoreType.DMA
@@ -1221,7 +1293,7 @@
             shape((288, 128), F32),
             shape((64, CHARS), F32),
         ),
-        in_specs=[vm] * 7,
+        in_specs=[vm] * 10,
         out_specs=(hbm, hbm, vm, vm, vm, vm),
         scratch_shapes=[
             pltpu.VMEM((HID, WIDE), BF16),
@@ -1244,6 +1316,15 @@
             pltpu.VMEM((3, 2, 64, CHARS), BF16),
             pltpu.VMEM((2, 64, CHARS), BF16),
             pltpu.VMEM((2, 64, CHARS), BF16),
+            pltpu.VMEM((ROWS, WIDE), BF16),
+            pltpu.VMEM((64, HID), BF16),
+            pltpu.VMEM((64, HID), BF16),
+            pltpu.VMEM((64, 128), jnp.int32),
+            pltpu.VMEM((64, CHARS), BF16),
+            pltpu.VMEM((CHARS, 128), F32),
+            pltpu.VMEM((8, CHARS), F32),
+            pltpu.VMEM((128, ROWS), F32),
+            pltpu.VMEM((128, 128), jnp.int32),
             dma((3, 5)),
             dma((3, 5)),
             dma((2, SLICES)),
@@ -1267,7 +1348,18 @@
         compiler_params=pltpu.CompilerParams(
             collective_id=0, has_side_effects=True, vmem_limit_bytes=60 * 2**20
         ),
-    )(wext, hidden_start.astype(BF16), cell_start.astype(BF16), meta, wout, table, dbias)
+    )(
+        char_ids.T,
+        targets.T,
+        hidden_start,
+        cell_start,
+        embedding,
+        input_weight.T,
+        hidden_weight,
+        gate_bias[None, :],
+        decoder_weight,
+        decoder_bias[None, :],
+    )
     grad, emb, norm, grad_hidden_start, grad_cell_start = pl.pallas_call(
         sum_kernel,
         out_shape=(
@@ -1311,28 +1403,55 @@
             collective_id=1, has_side_effects=True, vmem_limit_bytes=60 * 2**20
         ),
     )(dg.reshape(STEPS * ROWS, HID), hx.reshape(STEPS * ROWS, WIDE), dh0, dc0, emb, gdec_own)
-    grad_norm = jnp.sqrt(norm[0:1, 0])
-    factor = CLIP / jnp.maximum(grad_norm[0], CLIP)
     streams_all = streams * lax.axis_size("dp") * lax.axis_size("shard")
-    loss = emb[279, 0:1] / streams_all
-    grads = (
-        emb[:vocab, :INPUTS],
-        grad[:, HID : HID + INPUTS],
-        grad[:, :HID],
-        grad[:, HID + INPUTS],
-        gdec_own[:, :vocab],
-        emb[276:279].reshape(-1)[:vocab],
-    )
-    momenta = (
+    whole = lambda a: pl.BlockSpec(a, lambda n: (0, 0))
+    rows = lambda r, w: pl.BlockSpec((r, w), lambda n: (n, 0))
+    lanes = lambda r: pl.BlockSpec((r, ROWS // 2), lambda n: (0, n))
+    weights = [
+        (whole((vocab, INPUTS)), (vocab, INPUTS)),
+        (lanes(INPUTS), (INPUTS, ROWS)),
+        (rows(ROWS // 2, HID), (ROWS, HID)),
+        (lanes(1), (1, ROWS)),
+        (whole((64, vocab)), (64, vocab)),
+        (whole((1, vocab)), (1, vocab)),
+    ]
+    state = (rows(32, HID), (64, HID))
+    scalar = (pl.BlockSpec(memory_space=pltpu.SMEM), (1,))
+    results = [scalar, scalar, state, state] + weights + weights
+    loss, norm, gh, gc, *rest = pl.pallas_call(
+        functools.partial(finish_kernel, float(streams_all)),
+        grid=(2,),
+        out_shape=[shape(dims, F32) for _, dims in results],
+        in_specs=[
+            rows(ROWS // 2, WIDE),
+            whole((288, 128)),
+            whole((8, 128)),
+            whole((64, CHARS)),
+            state[0],
+            state[0],
+        ]
+        + [spec for spec, _ in weights],
+        out_specs=[spec for spec, _ in results],
+        compiler_params=pltpu.CompilerParams(vmem_limit_bytes=60 * 2**20),
+    )(
+        grad,
+        emb,
+        norm,
+        gdec_own,
+        grad_hidden_start,
+        grad_cell_start,
         momentum_embed,
-        momentum_input,
+        momentum_input.T,
         momentum_hidden,
-        momentum_gate,
+        momentum_gate[None, :],
         momentum_decoder,
-        momentum_outbias,
-    )
-    updated = tuple(MOMENTUM * momenta[n] + factor * grads[n] for n in range(6))
-    return (loss, grad_norm, grad_hidden_start, grad_cell_start) + grads + updated
+        momentum_outbias[None, :],
+    )
+    for n in (0, 6):
+        rest[n + 1] = rest[n + 1].T
+        rest[n + 3] = rest[n + 3].reshape(-1)
+        rest[n + 5] = rest[n + 5].reshape(-1)
+    return (loss, norm, gh, gc, *rest)
 
 
 def solution(mesh):

time: 288 us -> 271 us (0.941)
  local copies, waits for them, and re-layouts: 11.6 us -> 1.82 us
  other arithmetic: 11 us -> 2.48 us
  Pallas kernels: 257 us -> 262 us
  between operations: 4.79 us -> 0.91 us
    add x6 -> x0, other arithmetic: 7.74 us -> none  [split_local(): MOMENTUM * momenta[n] + factor * grads[n]]
    pallas_call x0 -> x1, Pallas kernels: none -> 4.8 us  [split_local(): pl.pallas_call(functools.partial(finish_kernel, float(streams_all)), grid...]
    unnamed x45 -> x2, local copies, waits for them, and re-layouts: 3.3 us -> 0.01 us
    convert_element_type x7 -> x0, other arithmetic: 3.25 us -> none  [the longest x1 1.76 us: split_local(): hidden_weight.astype(BF16)]
where the time goes in v1:
time: 271 us; the launch traced here: 267 us
  Pallas kernels  262 us (97%)
    pallas_call x1, Pallas kernels, split_local(): pl.pallas_call(step_kernel, out_shape=(shape((STEPS, ROWS, WIDE), BF16),...  172 us
    pallas_call x1, Pallas kernels, split_local(): pl.pallas_call(sum_kernel, out_shape=(shape((ROWS, WIDE), F32), shape((28...  84.9 us

profile of v1, /device:TPU:0, one launch (start us, length us, event | category | flops | bytes accessed | tf_op | source)
XLA Modules:
  0.0 267.4 jit_solution(12653446505614931668)
XLA Ops:
  0.6 1.2 broadcast_in_dim.13.outbias_in
  1.9 172.4 %shard_map.279 = (bf16[4,256,2176]{2,1,0:T(8,128)(2,1)}, bf16[4,256,2048]{2,1,0:T(8,128)(2,1)}, f32[256,2048]{1,0:T(8,128)}, f32[256,512]{1,0:T(8,128)}, f32[288,128]{1,0:T(8,128)}, /*index=5*/f32[64,384]{1,0:T(8,128)}) custom-call(s32[4,64]{1,0:T(4,128)} %bitcast.16, s32[4,64]{1,0:T(4,128)} %bitcast.17, f32[64,2048]{1,0:T(8,128)} %hidden_in.1, ...), custom_call_target="tpu_custom_call" | custom-call | tf_op jit(solution)/shard_map/pallas_call | solution.py:1286
  174.3 0.0 copy-start
  174.3 84.9 %shard_map.280 = (f32[256,2176]{1,0:T(8,128)}, f32[288,128]{1,0:T(8,128)}, f32[8,128]{1,0:T(8,128)}, f32[64,2048]{1,0:T(8,128)}, f32[64,2048]{1,0:T(8,128)}) custom-call(bf16[1024,2048]{1,0:T(8,128)(2,1)} %bitcast.13, bf16[1024,2176]{1,0:T(8,128)(2,1)} %bitcast.12, f32[256,2048]{1,0:T(8,128)} %get-tuple-element.45.dh0, f32[256,512]{1,0:T(8,128)} %get-tuple-element.46.dc0, ...), custom_call_target="tpu_custom_call" | custom-call | tf_op jit(solution)/shard_map/pallas_call | solution.py:1363
  259.3 0.0 copy-done
  259.3 0.6 broadcast_in_dim.15.m_outbias
  259.8 4.8 %shard_map.281 = (f32[1]{0:T(128)}, f32[1]{0:T(128)}, f32[64,2048]{1,0:T(8,128)}, f32[64,2048]{1,0:T(8,128)}, f32[275,100]{1,0:T(8,128)}, /*index=5*/f32[100,256...) custom-call(f32[256,2176]{1,0:T(8,128)} %get-tuple-element.49.grad, ...), custom_call_target="tpu_custom_call" | custom-call | tf_op jit(solution)/shard_map/pallas_call | solution.py:1421
  264.6 1.3 reduce
  265.9 1.2 reduce.1
Async XLA Ops:
  174.3 84.9 %copy-start = (f32[275]{0:T(512)S(1)}, f32[275]{0:T(512)}, u32[]{:S(2)}) copy-start(f32[275]{0:T(512)} %param.31) | copy-start | bytes 3304
